TPU v7x, 512 devices: a whole 4x8x8 slice. The times are simulated.
512 devices in a mesh: row: 4 (over z_lo, core), col: 16 (over x, z_hi), depth: 8 (over y).
Axes of the slice: x: 4, y: 8, z: 8 (z_hi: 4, z_lo: 2; z = z_hi * 2 + z_lo), core: 2. Of those that a mesh axis runs over, the one named last changes fastest.
Arguments:
- matrix: bfloat16 [8192, 8192], P('row', 'col'), may hold values from -6 to 6
- occupancy: int32 [128, 128], P('row', 'col'), may hold values 0 or 1
- filtering: int32 [128, 128], replicated, may hold values 0 or 1
Outputs:
- updated: bfloat16 [8192, 8192], P('row', ('col', 'depth'))
All inputs are finite; a program needn't handle non-finite values. No bound on the sum of `occupancy` on one device may be relied on, other than what follows from the above.
Results may differ from a plain program's by a relative error of at most 0.0095.
Values may be sent and summed in bfloat16 or wider, within the bound.
No kernel may reach another device: no remote copies, remote signals or barrier semaphores. Data moves between devices by JAX's collectives and lax.ppermute only.
A program may use at most 64 MiB of HBM per device.

v0:
```python
import functools

import jax
import jax.numpy as jnp
from jax import lax
from jax.experimental import pallas as pl
from jax.experimental.pallas import tpu as pltpu
from jax.sharding import PartitionSpec as P

BLK = 64
LANES = 128
RING = 4
ALONG_Z = [[x * RING + z for z in range(RING)] for x in range(RING)]
ALONG_X = [[x * RING + z for x in range(RING)] for z in range(RING)]
BF16 = jnp.bfloat16
F32 = jnp.float32
F16 = jnp.float16


def call(kernel, flops=0, moved=1 << 20, vmem=24 << 20, **kwargs):
    return pl.pallas_call(
        kernel,
        compiler_params=pltpu.CompilerParams(vmem_limit_bytes=vmem),
        cost_estimate=pl.CostEstimate(flops=flops, bytes_accessed=moved, transcendentals=0),
        **kwargs,
    )


def spread_tiles(occ_t, cols):
    tiles = occ_t.shape[0]
    tile = lax.broadcasted_iota(jnp.int32, (tiles, cols), 1) // BLK
    spread = (lax.broadcasted_iota(jnp.int32, (tiles, cols), 0) == tile).astype(F32)
    return lax.dot_general(
        occ_t.astype(F32), spread, (((0,), (0,)), ((), ())), preferred_element_type=F32
    )


def left_kernel(where, occ_t, rows, left, table):
    cycles, _, _, cols = rows.shape
    depths = table.shape[0] // cycles
    table[...] = spread_tiles(occ_t[...], cols)
    for a in range(cycles):
        mask = table[pl.ds(a * depths + where[0], 1), :]
        left[a * BLK : (a + 1) * BLK, :] = (rows[a, 0].astype(F32) * mask).astype(BF16)


def left_part(matrix, occupancy, where, depths):
    local_rows, cols = matrix.shape
    cycles = local_rows // (depths * BLK)
    occ_t = occupancy.T
    return call(
        left_kernel,
        vmem=60 << 20,
        out_shape=jax.ShapeDtypeStruct((cycles * BLK, cols), BF16),
        grid_spec=pltpu.PrefetchScalarGridSpec(
            num_scalar_prefetch=1,
            grid=(1,),
            in_specs=[
                pl.BlockSpec(occ_t.shape, lambda i, where: (0, 0)),
                pl.BlockSpec((cycles, 1, BLK, cols), lambda i, where: (0, where[0], 0, 0)),
            ],
            out_specs=pl.BlockSpec((cycles * BLK, cols), lambda i, where: (0, 0)),
            scratch_shapes=[pltpu.VMEM((cycles * depths, cols), F32)],
        ),
    )(where, occ_t, matrix.reshape(cycles, depths, BLK, cols))


def right_kernel(occ_t, rows, right):
    tiles, cols = rows.shape[0] // BLK, rows.shape[1]
    table = spread_tiles(occ_t[...], cols)
    for u in range(tiles):
        part = rows[u * BLK : (u + 1) * BLK, :].astype(F32)
        right[u * BLK : (u + 1) * BLK, :] = (part * table[u : u + 1, :]).astype(BF16)


def right_part(matrix, occupancy):
    return call(
        right_kernel, vmem=30 << 20, out_shape=jax.ShapeDtypeStruct(matrix.shape, BF16)
    )(occupancy.T, matrix)


def filter_kernel(depths, tile_rows, tile_cols, where, filtering, mask):
    rows, cols = mask.shape
    tiles = filtering.shape[0]
    row = lax.broadcasted_iota(jnp.int32, (rows, tiles), 0) // BLK * depths
    of_row = lax.broadcasted_iota(jnp.int32, (rows, tiles), 1) == (
        row + where[1] * tile_rows + where[0]
    )
    col = lax.broadcasted_iota(jnp.int32, (tiles, cols), 1) // BLK + where[2] * tile_cols
    of_col = lax.broadcasted_iota(jnp.int32, (tiles, cols), 0) == col
    spread = jnp.dot(of_row.astype(F32), filtering[...].astype(F32), preferred_element_type=F32)
    mask[...] = jnp.dot(spread, of_col.astype(F32), preferred_element_type=F32).astype(BF16)


def filter_mask(filtering, where, depths, tile_rows, tile_cols):
    shape = (tile_rows // depths * BLK, tile_cols * BLK)
    return call(
        functools.partial(filter_kernel, depths, tile_rows, tile_cols),
        out_shape=jax.ShapeDtypeStruct(shape, BF16),
        grid_spec=pltpu.PrefetchScalarGridSpec(
            num_scalar_prefetch=1,
            grid=(1,),
            in_specs=[pl.BlockSpec(filtering.shape, lambda i, where: (0, 0))],
            out_specs=pl.BlockSpec(shape, lambda i, where: (0, 0)),
        ),
    )(where, filtering)


def step_along_x(row):
    return (row & 1) * 2 + row // 2


def terms_kernel(held, scale, where, right, left, *outs):
    rows, inner = outs[0].shape[-2], left.shape[1]
    total = 0.0
    for a in range(RING):
        lefts = []
        for q in held:
            place = (where[1] + step_along_x(where[1] ^ q)) & (RING - 1)
            at = pl.multiple_of((place * RING + a) * rows, rows)
            lefts.append(left[pl.ds(at, rows), :])
        if len(right.shape) == 2:
            part = right[a * inner : (a + 1) * inner, :]
        else:
            part = [right[y, a * BLK : (a + 1) * BLK, :] for y in range(right.shape[0])]
            part = jnp.concatenate(part, axis=0)
        lefts = jnp.concatenate(lefts, axis=0)
        total = total + jnp.dot(lefts, part, preferred_element_type=F32)
    total = (scale * total).astype(BF16)
    for n in range(len(held)):
        part = total[n * rows : (n + 1) * rows]
        if len(outs[0].shape) == 3:
            outs[0][n] = part
        else:
            outs[n][...] = part


def terms_of(right, left, where, scale, rows, held, together):
    cols = right.shape[-1]
    vmem = pl.BlockSpec(memory_space=pltpu.VMEM)
    if together:
        out_shape = [jax.ShapeDtypeStruct((len(held), rows, cols), BF16)]
    else:
        out_shape = [jax.ShapeDtypeStruct((rows, cols), BF16)] * len(held)
    return call(
        functools.partial(terms_kernel, held, scale),
        flops=2 * rows * len(held) * RING * left.shape[1] * cols,
        moved=2 * (right.size + left.size // 2 + rows * len(held) * cols),
        out_shape=out_shape,
        in_specs=[pl.BlockSpec(memory_space=pltpu.SMEM), vmem, vmem],
        out_specs=[vmem] * len(out_shape),
    )(where, right, left)


def update_kernel(own, *refs):
    *terms, out = refs
    cube = 0.0
    for part in terms:
        cube = cube + part[...].astype(F32)
    out[...] = (1.5 * own[...].astype(F32) - 0.5 * cube).astype(BF16).T


def update(own, terms):
    shape = own.shape[::-1]
    return call(update_kernel, out_shape=jax.ShapeDtypeStruct(shape, BF16))(own, *terms)


def join_kernel(got, out):
    depths, _, lanes = got.shape
    low = lax.broadcasted_iota(jnp.int32, (BLK, LANES), 1) < BLK
    for d in range(0, depths, 2):
        for b in range(lanes // LANES):
            one, two = (got[d + s, :, b * LANES : (b + 1) * LANES].astype(F32) for s in (0, 1))
            even = jnp.where(low, one, pltpu.roll(two, BLK, 1))
            odd = jnp.where(low, pltpu.roll(one, BLK, 1), two)
            for a, value in ((2 * b, even), (2 * b + 1, odd)):
                at = (a * depths + d) * BLK
                out[:, at : at + LANES] = value.astype(BF16)


def join(got):
    depths, width, lanes = got.shape
    return call(join_kernel, out_shape=jax.ShapeDtypeStruct((width, depths * lanes), BF16))(got)


def shards(matrix, occupancy, filtering):
    rows = lax.axis_size("row")
    depths = lax.axis_size("depth")
    row, col, depth = (lax.axis_index(name) for name in ("row", "col", "depth"))
    local_rows, local_cols = matrix.shape
    own_rows = local_rows // depths
    scale = (local_rows * rows / 2.0) ** (-0.5)
    where = jnp.stack([depth, row, col]).astype(jnp.int32)

    def gather_col(value, groups):
        return lax.all_gather(value, "col", axis=0, tiled=True, axis_index_groups=groups)

    def swap_row(value, bit):
        return lax.ppermute(value, "row", [(r, r ^ bit) for r in range(rows)])

    def trade_x_and_row(value):
        places = [(r, x, z) for r in range(rows) for x in range(RING) for z in range(RING)]
        route = [
            ((r * RING + x) * RING + z, (x * RING + (x + step_along_x(r)) % RING) * RING + z)
            for r, x, z in places
        ]
        return lax.ppermute(value, ("row", "col"), route)

    def sum_over_row(right):
        [away] = terms_of(right, left, where, scale, own_rows, (1, 3), True)
        near, both = swap_row(away, 1)
        [across] = terms_of(right, left, where, scale, own_rows, (2,), False)
        across = swap_row((across.astype(F32) + both.astype(F32)).astype(BF16), 2)
        [here] = terms_of(right, left, where, scale, own_rows, (0,), False)
        return here, near, across

    own = left_part(matrix, occupancy, depth.astype(jnp.int32)[None], depths)
    moved = trade_x_and_row(own.astype(F16))
    right = right_part(matrix, occupancy)
    right, moved = lax.optimization_barrier((right, moved))
    left = gather_col(gather_col(moved, ALONG_Z), ALONG_X).astype(BF16)

    here, near, across = sum_over_row(right)
    here, later = lax.optimization_barrier((here, where))
    mask = filter_mask(filtering, later, depths, local_rows // BLK, local_cols // BLK)
    square = sum(part.astype(F32) for part in (here, near, across)) * mask.astype(F32)
    square = square.astype(BF16).astype(F16)
    squares = lax.all_gather(square, "depth", axis=0).astype(BF16)

    new = update(own, sum_over_row(squares)).reshape(depths, BLK, own_rows)
    return join(lax.all_to_all(new, "depth", 0, 0, tiled=True)).T


def solution(mesh):
    placed = (P("row", "col"), P("row", "col"), P())
    return jax.shard_map(
        shards, mesh=mesh, in_specs=placed, out_specs=P("row", ("col", "depth")), check_vma=False
    )
```

profile of v0, /device:TPU:6, one launch (start us, length us, event | category | flops | bytes accessed | tf_op | source)
XLA Modules:
  0.0 160.9 jit_solution(2394457118824153163)
XLA Ops:
  0.0 1.9 %shard_map.37.own = bf16[256,512]{1,0:T(8,128)(2,1)} custom-call(s32[1]{0:T(128)} %bitcast.where, s32[8,32]{1,0:T(8,128)} %bitcast.30, bf16[4,8,64,512]{3,2,1,0:T(8,128)(2,1)} %bitcast.28), custom_call_target="tpu_custom_call" | custom-call | bytes 1048576 | tf_op jit(solution)/shard_map/pallas_call | solution.py:51
  1.9 1.0 convert_element_type.54
  2.9 3.7 %collective-permute-start = (f16[256,512]{1,0:T(8,128)(2,1)S(1)}, f16[256,512]{1,0:T(8,128)(2,1)S(1)}, u32[]{:S(2)}, u32[]{:S(2)}) collective-permute-start(f16[256,512]{1,0:T(8,128)(2,1)S(1)} %convert_element_type.54), channel_id=1, source_target_pairs={{0,0},{8,8},{16,16},{24,24},{32,160},{40,168},{48,176},{56,184},{6... | collective-permute-start | bytes 786440 | tf_op jit(solution)/shard_map/ppermute | solution.py:207
  6.7 1.6 copy-done
  8.9 6.5 %collective-permute-done = f16[256,512]{1,0:T(8,128)(2,1)S(1)} collective-permute-done((f16[256,512]{1,0:T(8,128)(2,1)S(1)}, f16[256,512]{1,0:T(8,128)(2,1)S(1)}, u32[]{:S(2)}, u32[]{:S(2)}) %collective-permute-start) | collective-permute-done | bytes 262176 | tf_op jit(solution)/shard_map/ppermute | solution.py:207
  15.4 29.6 %all-gather.4 = f16[1024,512]{1,0:T(8,128)(2,1)S(1)} all-gather(f16[256,512]{1,0:T(8,128)(2,1)S(1)} %collective-permute-done), channel_id=1, replica_groups={{0,8,16,24},{32,40,48,56},{64,72,80,88},{96,104,112,120},{1,9,17,25},{3..., dimensions={0}, use_global_device_ids=true | all-gather | bytes 1310720 | tf_op jit(solution)/shard_map/all_gather | solution.py:196
  44.9 33.8 %all-gather.5 = f16[4096,512]{1,0:T(8,128)(2,1)S(1)} all-gather(f16[1024,512]{1,0:T(8,128)(2,1)S(1)} %all-gather.4), channel_id=1, replica_groups={{0,32,64,96},{8,40,72,104},{16,48,80,112},{24,56,88,120},{1,33,65,97},{..., dimensions={0}, use_global_device_ids=true | all-gather | bytes 5242880 | tf_op jit(solution)/shard_map/all_gather | solution.py:196
  78.7 0.8 convert_element_type.55.left
  79.5 1.8 %shard_map.40 = bf16[2,256,512]{2,1,0:T(8,128)(2,1)S(1)} custom-call(s32[3]{0:T(128)S(1)} %pad_add_fusion.where, bf16[2048,512]{1,0:T(8,128)(2,1)S(1)} %shard_map.38.right, bf16[4096,512]{1,0:T(8,128)(2,1)S(1)} %convert_element_type.55.left), custom_call_target="tpu_custom_call" | custom-call | flops 1073741824 | bytes 4718592 | tf_op jit(solution)/shard_map/pallas_call | solution.py:145
  81.3 1.9 %collective-permute-start.1 = (bf16[2,256,512]{2,1,0:T(8,128)(2,1)S(1)}, bf16[2,256,512]{2,1,0:T(8,128)(2,1)S(1)}, u32[]{:S(2)}, u32[]{:S(2)}) collective-permute-start(bf16[2,256,512]{2,1,0:T(8,128)(2,1)S(1)} %shard_map.40), channel_id=1, source_target_pairs={{0,128},{128,0},{256,384},{384,256},{1,129},{129,1},{257,385},{385... | collective-permute-start | bytes 1572872 | tf_op jit(solution)/shard_map/ppermute | solution.py:199
  83.3 1.2 shard_map.41
  85.2 2.1 %collective-permute-start.2 = (bf16[256,512]{1,0:T(8,128)(2,1)S(1)}, bf16[256,512]{1,0:T(8,128)(2,1)S(1)}, u32[]{:S(2)}, u32[]{:S(2)}) collective-permute-start(bf16[256,512]{1,0:T(8,128)(2,1)S(1)} %fusion.1), channel_id=1, source_target_pairs={{0,256},{128,384},{256,0},{384,128},{1,257},{129,385},{257,1},{385... | collective-permute-start | bytes 786440 | tf_op jit(solution)/shard_map/ppermute | solution.py:199
  87.3 1.2 shard_map.39
  88.5 0.9 shard_map.42
  89.4 6.2 %collective-permute-done.2 = bf16[256,512]{1,0:T(8,128)(2,1)S(1)} collective-permute-done((bf16[256,512]{1,0:T(8,128)(2,1)S(1)}, bf16[256,512]{1,0:T(8,128)(2,1)S(1)}, u32[]{:S(2)}, u32[]{:S(2)}) %collective-permute-start.2) | collective-permute-done | bytes 262176 | tf_op jit(solution)/shard_map/ppermute | solution.py:199
  95.7 31.5 %all-gather.6 = f16[2048,512]{1,0:T(8,128)(2,1)S(1)} all-gather(f16[256,512]{1,0:T(8,128)(2,1)S(1)} %fusion.5), channel_id=2, replica_groups=mesh['row'=4,'col'=16,'depth'=8] {'depth'}, dimensions={0}, use_global_device_ids=true | all-gather | bytes 2359296 | tf_op jit(solution)/shard_map/all_gather | solution.py:228
  127.7 1.8 %shard_map.44 = bf16[2,256,512]{2,1,0:T(8,128)(2,1)S(1)} custom-call(s32[3]{0:T(128)S(1)} %pad_add_fusion.where, bf16[8,256,512]{2,1,0:T(8,128)(2,1)S(1)} %bitcast.25, bf16[4096,512]{1,0:T(8,128)(2,1)S(1)} %convert_element_type.55.left), custom_call_target="tpu_custom_call" | custom-call | flops 1073741824 | bytes 4718592 | tf_op jit(solution)/shard_map/pallas_call | solution.py:145
  129.4 1.9 %collective-permute-start.3 = (bf16[2,256,512]{2,1,0:T(8,128)(2,1)S(1)}, bf16[2,256,512]{2,1,0:T(8,128)(2,1)S(1)}, u32[]{:S(2)}, u32[]{:S(2)}) collective-permute-start(bf16[2,256,512]{2,1,0:T(8,128)(2,1)S(1)} %shard_map.44), channel_id=1, source_target_pairs={{0,128},{128,0},{256,384},{384,256},{1,129},{129,1},{257,385},{385... | collective-permute-start | bytes 1572872 | tf_op jit(solution)/shard_map/ppermute | solution.py:199
  131.4 1.2 shard_map.45
  133.3 2.1 %collective-permute-start.4 = (bf16[256,512]{1,0:T(8,128)(2,1)S(1)}, bf16[256,512]{1,0:T(8,128)(2,1)S(1)}, u32[]{:S(2)}, u32[]{:S(2)}) collective-permute-start(bf16[256,512]{1,0:T(8,128)(2,1)S(1)} %fusion), channel_id=1, source_target_pairs={{0,256},{128,384},{256,0},{384,128},{1,257},{129,385},{257,1},{385... | collective-permute-start | bytes 786440 | tf_op jit(solution)/shard_map/ppermute | solution.py:199
  135.4 1.2 shard_map.43.refs_0_
  136.7 7.0 %collective-permute-done.4.refs_2_ = bf16[256,512]{1,0:T(8,128)(2,1)S(1)} collective-permute-done((bf16[256,512]{1,0:T(8,128)(2,1)S(1)}, bf16[256,512]{1,0:T(8,128)(2,1)S(1)}, u32[]{:S(2)}, u32[]{:S(2)}) %collective-permute-start.4) | collective-permute-done | bytes 262176 | tf_op jit(solution)/shard_map/ppermute | solution.py:199
  143.9 16.1 %all_to_all.5.got = bf16[8,64,256]{2,1,0:T(8,128)(2,1)S(1)} all-to-all(bf16[8,64,256]{2,1,0:T(8,128)(2,1)S(1)} %bitcast.29), channel_id=1, replica_groups=mesh['row'=4,'col'=16,'depth'=8] {'depth'}, dimensions={0} | all-to-all | bytes 524288 | tf_op jit(solution)/shard_map/all_to_all | solution.py:231
  160.0 0.8 shard_map.47
  (17 shorter events, 2.8 us)
Async XLA Ops:
  0.0 6.6 %copy-start.3 = (s32[32,8]{0,1:T(8,128)S(1)}, s32[32,8]{0,1:T(8,128)}, u32[]{:S(2)}) copy-start(s32[32,8]{0,1:T(8,128)} %param.4) | copy-start | bytes 3076
  2.9 12.4 %collective-permute-start = (f16[256,512]{1,0:T(8,128)(2,1)S(1)}, f16[256,512]{1,0:T(8,128)(2,1)S(1)}, u32[]{:S(2)}, u32[]{:S(2)}) collective-permute-start(f16[256,512]{1,0:T(8,128)(2,1)S(1)} %convert_element_type.54), channel_id=1, source_target_pairs={{0,0},{8,8},{16,16},{24,24},{32,160},{40,168},{48,176},{56,184},{6... | collective-permute-start | bytes 786440 | tf_op jit(solution)/shard_map/ppermute | solution.py:207
  6.7 1.6 copy-start
  81.3 3.8 %collective-permute-start.1 = (bf16[2,256,512]{2,1,0:T(8,128)(2,1)S(1)}, bf16[2,256,512]{2,1,0:T(8,128)(2,1)S(1)}, u32[]{:S(2)}, u32[]{:S(2)}) collective-permute-start(bf16[2,256,512]{2,1,0:T(8,128)(2,1)S(1)} %shard_map.40), channel_id=1, source_target_pairs={{0,128},{128,0},{256,384},{384,256},{1,129},{129,1},{257,385},{385... | collective-permute-start | bytes 1572872 | tf_op jit(solution)/shard_map/ppermute | solution.py:199
  85.2 3.3 %copy-start.2 = (s32[128,128]{1,0:T(8,128)S(1)}, s32[128,128]{1,0:T(8,128)}, u32[]{:S(2)}) copy-start(s32[128,128]{1,0:T(8,128)} %filtering.1) | copy-start | bytes 196612
  85.2 10.4 %collective-permute-start.2 = (bf16[256,512]{1,0:T(8,128)(2,1)S(1)}, bf16[256,512]{1,0:T(8,128)(2,1)S(1)}, u32[]{:S(2)}, u32[]{:S(2)}) collective-permute-start(bf16[256,512]{1,0:T(8,128)(2,1)S(1)} %fusion.1), channel_id=1, source_target_pairs={{0,256},{128,384},{256,0},{384,128},{1,257},{129,385},{257,1},{385... | collective-permute-start | bytes 786440 | tf_op jit(solution)/shard_map/ppermute | solution.py:199
  129.4 3.8 %collective-permute-start.3 = (bf16[2,256,512]{2,1,0:T(8,128)(2,1)S(1)}, bf16[2,256,512]{2,1,0:T(8,128)(2,1)S(1)}, u32[]{:S(2)}, u32[]{:S(2)}) collective-permute-start(bf16[2,256,512]{2,1,0:T(8,128)(2,1)S(1)} %shard_map.44), channel_id=1, source_target_pairs={{0,128},{128,0},{256,384},{384,256},{1,129},{129,1},{257,385},{385... | collective-permute-start | bytes 1572872 | tf_op jit(solution)/shard_map/ppermute | solution.py:199
  133.3 10.4 %copy-start.1 = (bf16[256,512]{1,0:T(8,128)(2,1)S(1)}, bf16[256,512]{1,0:T(8,128)(2,1)}, u32[]{:S(2)}) copy-start(bf16[256,512]{1,0:T(8,128)(2,1)} %shard_map.37.own) | copy-start | bytes 786436
  133.3 10.4 %collective-permute-start.4 = (bf16[256,512]{1,0:T(8,128)(2,1)S(1)}, bf16[256,512]{1,0:T(8,128)(2,1)S(1)}, u32[]{:S(2)}, u32[]{:S(2)}) collective-permute-start(bf16[256,512]{1,0:T(8,128)(2,1)S(1)} %fusion), channel_id=1, source_target_pairs={{0,256},{128,384},{256,0},{384,128},{1,257},{129,385},{257,1},{385... | collective-permute-start | bytes 786440 | tf_op jit(solution)/shard_map/ppermute | solution.py:199
where the time goes:
time: 161 us
  blocking collectives  111 us (69%)
  waiting for transfers between devices  21 us (13%)
  Pallas kernels  12.9 us (8%)
  starting transfers between devices  11.7 us (7%)
  other arithmetic  2.6 us (2%)
  local copies, waits for them, and re-layouts  1.62 us (1%)
    all_gather x2, blocking collectives, gather_col(): lax.all_gather(value, 'col', axis=0, tiled=True, axis_index_groups=groups)  63.3 us
    all_gather x1, blocking collectives, shards(): squares = lax.all_gather(square, 'depth', axis=0).astype(BF16)  31.5 us
    all_to_all x1, blocking collectives, shards(): return join(lax.all_to_all(new, 'depth', 0, 0, tiled=True)).T  16.1 us
    ppermute x4, waiting for transfers between devices, swap_row(): return lax.ppermute(value, 'row', [(r, r ^ bit) for r in range(rows)])  14.5 us
    pallas_call x6, Pallas kernels, terms_of(): call(functools.partial(terms_kernel, held, scale), flops=2 * rows * len(h...  8.54 us
    ppermute x4, starting transfers between devices, swap_row(): return lax.ppermute(value, 'row', [(r, r ^ bit) for r in range(rows)])  7.95 us
    ppermute x1, waiting for transfers between devices, trade_x_and_row(): return lax.ppermute(value, ('row', 'col'), route)  6.48 us
    ppermute x1, starting transfers between devices, trade_x_and_row(): return lax.ppermute(value, ('row', 'col'), route)  3.72 us
  transfers between devices with their start and end apart: 5, of which 5 were waited for; matrix products, arithmetic and copies ran while one was open for 0% of the time, Pallas kernels for 4%

commit v1 on v0

--- a/solution.py
+++ b/solution.py
@@ -127,21 +127,14 @@
         lefts = jnp.concatenate(lefts, axis=0)
         total = total + jnp.dot(lefts, part, preferred_element_type=F32)
     total = (scale * total).astype(BF16)
-    for n in range(len(held)):
-        part = total[n * rows : (n + 1) * rows]
-        if len(outs[0].shape) == 3:
-            outs[0][n] = part
-        else:
-            outs[n][...] = part
-
-
-def terms_of(right, left, where, scale, rows, held, together):
+    for n, out in enumerate(outs):
+        out[...] = total[n * rows : (n + 1) * rows]
+
+
+def terms_of(right, left, where, scale, rows, held):
     cols = right.shape[-1]
     vmem = pl.BlockSpec(memory_space=pltpu.VMEM)
-    if together:
-        out_shape = [jax.ShapeDtypeStruct((len(held), rows, cols), BF16)]
-    else:
-        out_shape = [jax.ShapeDtypeStruct((rows, cols), BF16)] * len(held)
+    out_shape = [jax.ShapeDtypeStruct((rows, cols), BF16)] * len(held)
     return call(
         functools.partial(terms_kernel, held, scale),
         flops=2 * rows * len(held) * RING * left.shape[1] * cols,
@@ -207,23 +200,25 @@
         return lax.ppermute(value, ("row", "col"), route)
 
     def sum_over_row(right):
-        [away] = terms_of(right, left, where, scale, own_rows, (1, 3), True)
-        near, both = swap_row(away, 1)
-        [across] = terms_of(right, left, where, scale, own_rows, (2,), False)
-        across = swap_row((across.astype(F32) + both.astype(F32)).astype(BF16), 2)
-        [here] = terms_of(right, left, where, scale, own_rows, (0,), False)
-        return here, near, across
+        [both] = terms_of(right, left, where, scale, own_rows, (3,))
+        both = swap_row(both, 1)
+        [across] = terms_of(right, left, where, scale, own_rows, (2,))
+        across = (across.astype(F32) + both.astype(F32)).astype(BF16)
+        across, later = lax.optimization_barrier((across, where))
+        across = swap_row(across, 2)
+        near, here = terms_of(right, left, later, scale, own_rows, (1, 0))
+        across, here = lax.optimization_barrier((across, here))
+        return here, across, swap_row(near, 1)
 
     own = left_part(matrix, occupancy, depth.astype(jnp.int32)[None], depths)
     moved = trade_x_and_row(own.astype(F16))
     right = right_part(matrix, occupancy)
-    right, moved = lax.optimization_barrier((right, moved))
+    mask = filter_mask(filtering, where, depths, local_rows // BLK, local_cols // BLK)
+    right, mask, moved = lax.optimization_barrier((right, mask, moved))
     left = gather_col(gather_col(moved, ALONG_Z), ALONG_X).astype(BF16)
 
-    here, near, across = sum_over_row(right)
-    here, later = lax.optimization_barrier((here, where))
-    mask = filter_mask(filtering, later, depths, local_rows // BLK, local_cols // BLK)
-    square = sum(part.astype(F32) for part in (here, near, across)) * mask.astype(F32)
+    here, across, near = sum_over_row(right)
+    square = sum(part.astype(F32) for part in (here, across, near)) * mask.astype(F32)
     square = square.astype(BF16).astype(F16)
     squares = lax.all_gather(square, "depth", axis=0).astype(BF16)
 

time: 161 us -> 160 us (level)
  waiting for transfers between devices: 21 us -> 14.8 us
  starting transfers between devices: 11.7 us -> 15.9 us
    ppermute x4 -> x6, waiting for transfers between devices: 14.5 us -> 9.45 us  [swap_row(): return lax.ppermute(value, 'row', [(r, r ^ bit) for r in range(rows)])]
    ppermute x4 -> x6, starting transfers between devices: 7.95 us -> 12.1 us  [swap_row(): return lax.ppermute(value, 'row', [(r, r ^ bit) for r in range(rows)])]
  transfers between devices with their start and end apart: 5 -> 7, of which waited for: 5 -> 5; matrix products, arithmetic and copies ran while one was open for 0% -> 0% of each run, Pallas kernels for 4% -> 5%
where the time goes in v1:
time: 160 us; the launch traced here: 159 us
  blocking collectives  111 us (69%)
  starting transfers between devices  15.9 us (10%)
  waiting for transfers between devices  14.8 us (9%)
  Pallas kernels  12.9 us (8%)
  other arithmetic  2.6 us (2%)
  local copies, waits for them, and re-layouts  1.81 us (1%)
    all_gather x2, blocking collectives, gather_col(): lax.all_gather(value, 'col', axis=0, tiled=True, axis_index_groups=groups)  63.4 us
    all_gather x1, blocking collectives, shards(): squares = lax.all_gather(square, 'depth', axis=0).astype(BF16)  31.2 us
    all_to_all x1, blocking collectives, shards(): return join(lax.all_to_all(new, 'depth', 0, 0, tiled=True)).T  16.6 us
    ppermute x6, starting transfers between devices, swap_row(): return lax.ppermute(value, 'row', [(r, r ^ bit) for r in range(rows)])  12.1 us
    ppermute x6, waiting for transfers between devices, swap_row(): return lax.ppermute(value, 'row', [(r, r ^ bit) for r in range(rows)])  9.45 us
    pallas_call x6, Pallas kernels, terms_of(): call(functools.partial(terms_kernel, held, scale), flops=2 * rows * len(h...  8.54 us
    ppermute x1, waiting for transfers between devices, trade_x_and_row(): return lax.ppermute(value, ('row', 'col'), route)  5.4 us
    ppermute x1, starting transfers between devices, trade_x_and_row(): return lax.ppermute(value, ('row', 'col'), route)  3.72 us
  transfers between devices with their start and end apart: 7, of which 5 were waited for; matrix products, arithmetic and copies ran while one was open for 0% of the time, Pallas kernels for 5%

profile of v1, /device:TPU:6, one launch (start us, length us, event | category | flops | bytes accessed | tf_op | source)
XLA Modules:
  0.0 159.4 jit_solution(18053093659401132570)
XLA Ops:
  0.0 1.9 %shard_map.37.own = bf16[256,512]{1,0:T(8,128)(2,1)} custom-call(s32[1]{0:T(128)} %bitcast.where, s32[8,32]{1,0:T(8,128)} %bitcast.13, bf16[4,8,64,512]{3,2,1,0:T(8,128)(2,1)} %bitcast.11), custom_call_target="tpu_custom_call" | custom-call | bytes 1048576 | tf_op jit(solution)/shard_map/pallas_call | solution.py:51
  1.9 1.0 convert_element_type.45
  2.9 3.7 %collective-permute-start = (f16[256,512]{1,0:T(8,128)(2,1)S(1)}, f16[256,512]{1,0:T(8,128)(2,1)S(1)}, u32[]{:S(2)}, u32[]{:S(2)}) collective-permute-start(f16[256,512]{1,0:T(8,128)(2,1)S(1)} %convert_element_type.45), channel_id=1, source_target_pairs={{0,0},{8,8},{16,16},{24,24},{32,160},{40,168},{48,176},{56,184},{6... | collective-permute-start | bytes 786440 | tf_op jit(solution)/shard_map/ppermute | solution.py:200
  6.7 1.6 copy-done
  9.1 0.9 shard_map.39
  10.0 5.4 %collective-permute-done = f16[256,512]{1,0:T(8,128)(2,1)S(1)} collective-permute-done((f16[256,512]{1,0:T(8,128)(2,1)S(1)}, f16[256,512]{1,0:T(8,128)(2,1)S(1)}, u32[]{:S(2)}, u32[]{:S(2)}) %collective-permute-start) | collective-permute-done | bytes 262176 | tf_op jit(solution)/shard_map/ppermute | solution.py:200
  15.4 30.1 %all-gather.4 = f16[1024,512]{1,0:T(8,128)(2,1)S(1)} all-gather(f16[256,512]{1,0:T(8,128)(2,1)S(1)} %collective-permute-done), channel_id=1, replica_groups={{0,8,16,24},{32,40,48,56},{64,72,80,88},{96,104,112,120},{1,9,17,25},{3..., dimensions={0}, use_global_device_ids=true | all-gather | bytes 1310720 | tf_op jit(solution)/shard_map/all_gather | solution.py:189
  45.5 33.2 %all-gather.5 = f16[4096,512]{1,0:T(8,128)(2,1)S(1)} all-gather(f16[1024,512]{1,0:T(8,128)(2,1)S(1)} %all-gather.4), channel_id=1, replica_groups={{0,32,64,96},{8,40,72,104},{16,48,80,112},{24,56,88,120},{1,33,65,97},{..., dimensions={0}, use_global_device_ids=true | all-gather | bytes 5242880 | tf_op jit(solution)/shard_map/all_gather | solution.py:189
  79.6 1.2 shard_map.41
  80.8 1.9 %collective-permute-start.1 = (bf16[256,512]{1,0:T(8,128)(2,1)S(1)}, bf16[256,512]{1,0:T(8,128)(2,1)S(1)}, u32[]{:S(2)}, u32[]{:S(2)}) collective-permute-start(bf16[256,512]{1,0:T(8,128)(2,1)S(1)} %shard_map.41), channel_id=1, source_target_pairs={{0,128},{128,0},{256,384},{384,256},{1,129},{129,1},{257,385},{385... | collective-permute-start | bytes 786440 | tf_op jit(solution)/shard_map/ppermute | solution.py:192
  82.7 1.2 shard_map.40
  84.3 1.9 %collective-permute-start.2 = (bf16[256,512]{1,0:T(8,128)(2,1)S(1)}, bf16[256,512]{1,0:T(8,128)(2,1)S(1)}, u32[]{:S(2)}, u32[]{:S(2)}) collective-permute-start(bf16[256,512]{1,0:T(8,128)(2,1)S(1)} %add_convert_fusion.1), channel_id=1, source_target_pairs={{0,256},{128,384},{256,0},{384,128},{1,257},{129,385},{257,1},{385... | collective-permute-start | bytes 786440 | tf_op jit(solution)/shard_map/ppermute | solution.py:192
  86.2 1.8 %shard_map.42 = (bf16[256,512]{1,0:T(8,128)(2,1)S(1)}, bf16[256,512]{1,0:T(8,128)(2,1)S(1)}) custom-call(s32[3]{0:T(128)S(1)} %pad_add_fusion.where, bf16[2048,512]{1,0:T(8,128)(2,1)S(1)} %shard_map.38.right, bf16[4096,512]{1,0:T(8,128)(2,1)S(1)} %convert_element_type.46.left), custom_call_target="tpu_custom_call" | custom-call | flops 1073741824 | bytes 4718592 | tf_op jit(solution)/shard_map/pallas_call | solution.py:138
  88.0 2.2 %collective-permute-start.3 = (bf16[256,512]{1,0:T(8,128)(2,1)S(1)}, bf16[256,512]{1,0:T(8,128)(2,1)S(1)}, u32[]{:S(2)}, u32[]{:S(2)}) collective-permute-start(bf16[256,512]{1,0:T(8,128)(2,1)S(1)} %get-tuple-element.27), channel_id=1, source_target_pairs={{0,128},{128,0},{256,384},{384,256},{1,129},{129,1},{257,385},{385... | collective-permute-start | bytes 786440 | tf_op jit(solution)/shard_map/ppermute | solution.py:192
  90.2 4.5 %collective-permute-done.2 = bf16[256,512]{1,0:T(8,128)(2,1)S(1)} collective-permute-done((bf16[256,512]{1,0:T(8,128)(2,1)S(1)}, bf16[256,512]{1,0:T(8,128)(2,1)S(1)}, u32[]{:S(2)}, u32[]{:S(2)}) %collective-permute-start.2) | collective-permute-done | bytes 262176 | tf_op jit(solution)/shard_map/ppermute | solution.py:192
  94.8 31.2 %all-gather.6 = f16[2048,512]{1,0:T(8,128)(2,1)S(1)} all-gather(f16[256,512]{1,0:T(8,128)(2,1)S(1)} %fusion), channel_id=2, replica_groups=mesh['row'=4,'col'=16,'depth'=8] {'depth'}, dimensions={0}, use_global_device_ids=true | all-gather | bytes 2359296 | tf_op jit(solution)/shard_map/all_gather | solution.py:223
  126.5 1.2 shard_map.44
  127.7 1.9 %collective-permute-start.4 = (bf16[256,512]{1,0:T(8,128)(2,1)S(1)}, bf16[256,512]{1,0:T(8,128)(2,1)S(1)}, u32[]{:S(2)}, u32[]{:S(2)}) collective-permute-start(bf16[256,512]{1,0:T(8,128)(2,1)S(1)} %shard_map.44), channel_id=1, source_target_pairs={{0,128},{128,0},{256,384},{384,256},{1,129},{129,1},{257,385},{385... | collective-permute-start | bytes 786440 | tf_op jit(solution)/shard_map/ppermute | solution.py:192
  129.6 1.2 shard_map.43
  131.2 2.2 %collective-permute-start.5 = (bf16[256,512]{1,0:T(8,128)(2,1)S(1)}, bf16[256,512]{1,0:T(8,128)(2,1)S(1)}, u32[]{:S(2)}, u32[]{:S(2)}) collective-permute-start(bf16[256,512]{1,0:T(8,128)(2,1)S(1)} %add_convert_fusion), channel_id=1, source_target_pairs={{0,256},{128,384},{256,0},{384,128},{1,257},{129,385},{257,1},{385... | collective-permute-start | bytes 786440 | tf_op jit(solution)/shard_map/ppermute | solution.py:192
  133.4 1.8 %shard_map.45 = (bf16[256,512]{1,0:T(8,128)(2,1)S(1)}, bf16[256,512]{1,0:T(8,128)(2,1)S(1)}) custom-call(s32[3]{0:T(128)S(1)} %pad_add_fusion.where, bf16[8,256,512]{2,1,0:T(8,128)(2,1)S(1)} %bitcast.10, bf16[4096,512]{1,0:T(8,128)(2,1)S(1)} %convert_element_type.46.left), custom_call_target="tpu_custom_call" | custom-call | flops 1073741824 | bytes 4718592 | tf_op jit(solution)/shard_map/pallas_call | solution.py:138
  135.2 2.1 %collective-permute-start.6 = (bf16[256,512]{1,0:T(8,128)(2,1)S(1)}, bf16[256,512]{1,0:T(8,128)(2,1)S(1)}, u32[]{:S(2)}, u32[]{:S(2)}) collective-permute-start(bf16[256,512]{1,0:T(8,128)(2,1)S(1)} %get-tuple-element.34), channel_id=1, source_target_pairs={{0,128},{128,0},{256,384},{384,256},{1,129},{129,1},{257,385},{385... | collective-permute-start | bytes 786440 | tf_op jit(solution)/shard_map/ppermute | solution.py:192
  137.2 4.5 %collective-permute-done.5.refs_1_ = bf16[256,512]{1,0:T(8,128)(2,1)S(1)} collective-permute-done((bf16[256,512]{1,0:T(8,128)(2,1)S(1)}, bf16[256,512]{1,0:T(8,128)(2,1)S(1)}, u32[]{:S(2)}, u32[]{:S(2)}) %collective-permute-start.5) | collective-permute-done | bytes 262176 | tf_op jit(solution)/shard_map/ppermute | solution.py:192
  141.9 16.6 %all_to_all.5.got = bf16[8,64,256]{2,1,0:T(8,128)(2,1)S(1)} all-to-all(bf16[8,64,256]{2,1,0:T(8,128)(2,1)S(1)} %bitcast.12), channel_id=1, replica_groups=mesh['row'=4,'col'=16,'depth'=8] {'depth'}, dimensions={0} | all-to-all | bytes 524288 | tf_op jit(solution)/shard_map/all_to_all | solution.py:226
  (20 shorter events, 3.9 us)
Async XLA Ops:
  0.0 6.6 %copy-start.3 = (s32[32,8]{0,1:T(8,128)S(1)}, s32[32,8]{0,1:T(8,128)}, u32[]{:S(2)}) copy-start(s32[32,8]{0,1:T(8,128)} %param.4) | copy-start | bytes 3076
  2.9 12.4 %collective-permute-start = (f16[256,512]{1,0:T(8,128)(2,1)S(1)}, f16[256,512]{1,0:T(8,128)(2,1)S(1)}, u32[]{:S(2)}, u32[]{:S(2)}) collective-permute-start(f16[256,512]{1,0:T(8,128)(2,1)S(1)} %convert_element_type.45), channel_id=1, source_target_pairs={{0,0},{8,8},{16,16},{24,24},{32,160},{40,168},{48,176},{56,184},{6... | collective-permute-start | bytes 786440 | tf_op jit(solution)/shard_map/ppermute | solution.py:200
  6.7 1.6 %copy-start = (bf16[2048,512]{1,0:T(8,128)(2,1)S(1)}, bf16[2048,512]{1,0:T(8,128)(2,1)}, u32[]{:S(2)}) copy-start(bf16[2048,512]{1,0:T(8,128)(2,1)} %rows.1) | copy-start | bytes 6291460
  8.2 0.8 copy-start.2
  80.8 3.4 %collective-permute-start.1 = (bf16[256,512]{1,0:T(8,128)(2,1)S(1)}, bf16[256,512]{1,0:T(8,128)(2,1)S(1)}, u32[]{:S(2)}, u32[]{:S(2)}) collective-permute-start(bf16[256,512]{1,0:T(8,128)(2,1)S(1)} %shard_map.41), channel_id=1, source_target_pairs={{0,128},{128,0},{256,384},{384,256},{1,129},{129,1},{257,385},{385... | collective-permute-start | bytes 786440 | tf_op jit(solution)/shard_map/ppermute | solution.py:192
  84.3 10.4 %collective-permute-start.2 = (bf16[256,512]{1,0:T(8,128)(2,1)S(1)}, bf16[256,512]{1,0:T(8,128)(2,1)S(1)}, u32[]{:S(2)}, u32[]{:S(2)}) collective-permute-start(bf16[256,512]{1,0:T(8,128)(2,1)S(1)} %add_convert_fusion.1), channel_id=1, source_target_pairs={{0,256},{128,384},{256,0},{384,128},{1,257},{129,385},{257,1},{385... | collective-permute-start | bytes 786440 | tf_op jit(solution)/shard_map/ppermute | solution.py:192
  88.0 6.6 %collective-permute-start.3 = (bf16[256,512]{1,0:T(8,128)(2,1)S(1)}, bf16[256,512]{1,0:T(8,128)(2,1)S(1)}, u32[]{:S(2)}, u32[]{:S(2)}) collective-permute-start(bf16[256,512]{1,0:T(8,128)(2,1)S(1)} %get-tuple-element.27), channel_id=1, source_target_pairs={{0,128},{128,0},{256,384},{384,256},{1,129},{129,1},{257,385},{385... | collective-permute-start | bytes 786440 | tf_op jit(solution)/shard_map/ppermute | solution.py:192
  127.7 3.4 %collective-permute-start.4 = (bf16[256,512]{1,0:T(8,128)(2,1)S(1)}, bf16[256,512]{1,0:T(8,128)(2,1)S(1)}, u32[]{:S(2)}, u32[]{:S(2)}) collective-permute-start(bf16[256,512]{1,0:T(8,128)(2,1)S(1)} %shard_map.44), channel_id=1, source_target_pairs={{0,128},{128,0},{256,384},{384,256},{1,129},{129,1},{257,385},{385... | collective-permute-start | bytes 786440 | tf_op jit(solution)/shard_map/ppermute | solution.py:192
  131.2 10.5 %copy-start.1 = (bf16[256,512]{1,0:T(8,128)(2,1)S(1)}, bf16[256,512]{1,0:T(8,128)(2,1)}, u32[]{:S(2)}) copy-start(bf16[256,512]{1,0:T(8,128)(2,1)} %shard_map.37.own) | copy-start | bytes 786436
  131.2 10.5 %collective-permute-start.5 = (bf16[256,512]{1,0:T(8,128)(2,1)S(1)}, bf16[256,512]{1,0:T(8,128)(2,1)S(1)}, u32[]{:S(2)}, u32[]{:S(2)}) collective-permute-start(bf16[256,512]{1,0:T(8,128)(2,1)S(1)} %add_convert_fusion), channel_id=1, source_target_pairs={{0,256},{128,384},{256,0},{384,128},{1,257},{129,385},{257,1},{385... | collective-permute-start | bytes 786440 | tf_op jit(solution)/shard_map/ppermute | solution.py:192
  135.2 6.5 %collective-permute-start.6 = (bf16[256,512]{1,0:T(8,128)(2,1)S(1)}, bf16[256,512]{1,0:T(8,128)(2,1)S(1)}, u32[]{:S(2)}, u32[]{:S(2)}) collective-permute-start(bf16[256,512]{1,0:T(8,128)(2,1)S(1)} %get-tuple-element.34), channel_id=1, source_target_pairs={{0,128},{128,0},{256,384},{384,256},{1,129},{129,1},{257,385},{385... | collective-permute-start | bytes 786440 | tf_op jit(solution)/shard_map/ppermute | solution.py:192

commit v2 on v1

--- a/solution.py
+++ b/solution.py
@@ -127,14 +127,20 @@
         lefts = jnp.concatenate(lefts, axis=0)
         total = total + jnp.dot(lefts, part, preferred_element_type=F32)
     total = (scale * total).astype(BF16)
-    for n, out in enumerate(outs):
-        out[...] = total[n * rows : (n + 1) * rows]
-
-
-def terms_of(right, left, where, scale, rows, held):
+    for n in range(len(held)):
+        part = total[n * rows : (n + 1) * rows]
+        if len(outs) == len(held):
+            outs[n][...] = part
+        else:
+            outs[0][n] = part
+
+
+def terms_of(right, left, where, scale, rows, held, together=False):
     cols = right.shape[-1]
     vmem = pl.BlockSpec(memory_space=pltpu.VMEM)
     out_shape = [jax.ShapeDtypeStruct((rows, cols), BF16)] * len(held)
+    if together:
+        out_shape = [jax.ShapeDtypeStruct((len(held), rows, cols), BF16)]
     return call(
         functools.partial(terms_kernel, held, scale),
         flops=2 * rows * len(held) * RING * left.shape[1] * cols,
@@ -145,35 +151,74 @@
     )(where, right, left)
 
 
-def update_kernel(own, *refs):
-    *terms, out = refs
-    cube = 0.0
-    for part in terms:
-        cube = cube + part[...].astype(F32)
-    out[...] = (1.5 * own[...].astype(F32) - 0.5 * cube).astype(BF16).T
-
-
-def update(own, terms):
-    shape = own.shape[::-1]
-    return call(update_kernel, out_shape=jax.ShapeDtypeStruct(shape, BF16))(own, *terms)
-
-
-def join_kernel(got, out):
-    depths, _, lanes = got.shape
+def pack_kernel(where, here, near, across, both, out):
+    mine = (here[...].astype(F32) + near[...].astype(F32)).astype(BF16).T
+    other = (across[...].astype(F32) + both[...].astype(F32)).astype(BF16).T
+    first = where[1] < 2
+    out[0] = jnp.where(first, mine, other)
+    out[1] = jnp.where(first, other, mine)
+
+
+def pack(parts, where):
+    rows, cols = parts[0].shape
+    vmem = pl.BlockSpec(memory_space=pltpu.VMEM)
+    return call(
+        pack_kernel,
+        out_shape=jax.ShapeDtypeStruct((2, cols, rows), BF16),
+        in_specs=[pl.BlockSpec(memory_space=pltpu.SMEM)] + [vmem] * len(parts),
+        out_specs=vmem,
+    )(where, *parts)
+
+
+def own_kernel(where, occ_t, columns, own):
+    tiles, _, _ = columns.shape
+    turned = jnp.concatenate([columns[t] for t in range(tiles)], axis=0).T
+    low = lax.rem(where[0], 2) == 0
+    mine = jnp.where(low, turned[:BLK, :].astype(F32), turned[BLK:, :].astype(F32))
+    row = lax.broadcasted_iota(jnp.int32, (1, tiles * BLK), 1) // BLK
+    mask = jnp.zeros((1, tiles * BLK), F32)
+    for t in range(tiles):
+        mask = jnp.where(row == t, occ_t[where[0], t].astype(F32), mask)
+    own[...] = (mine * mask).astype(BF16)
+
+
+def own_columns(matrix, occupancy, where):
+    local_rows, local_cols = matrix.shape
+    tiles = local_rows // BLK
+    return call(
+        own_kernel,
+        out_shape=jax.ShapeDtypeStruct((BLK, local_rows), BF16),
+        grid_spec=pltpu.PrefetchScalarGridSpec(
+            num_scalar_prefetch=2,
+            grid=(1,),
+            in_specs=[
+                pl.BlockSpec((tiles, BLK, LANES), lambda i, where, occ: (0, 0, where[0] // 2))
+            ],
+            out_specs=pl.BlockSpec((BLK, local_rows), lambda i, where, occ: (0, 0)),
+        ),
+    )(where, occupancy.T, matrix.reshape(tiles, BLK, local_cols))
+
+
+def update_kernel(own, got, out):
+    depths, lanes = got.shape[0] // 2, got.shape[2]
     low = lax.broadcasted_iota(jnp.int32, (BLK, LANES), 1) < BLK
     for d in range(0, depths, 2):
         for b in range(lanes // LANES):
-            one, two = (got[d + s, :, b * LANES : (b + 1) * LANES].astype(F32) for s in (0, 1))
+            span = slice(b * LANES, (b + 1) * LANES)
+            one, two = (
+                got[d + s, :, span].astype(F32) + got[depths + d + s, :, span].astype(F32)
+                for s in (0, 1)
+            )
             even = jnp.where(low, one, pltpu.roll(two, BLK, 1))
             odd = jnp.where(low, pltpu.roll(one, BLK, 1), two)
-            for a, value in ((2 * b, even), (2 * b + 1, odd)):
+            for a, cube in ((2 * b, even), (2 * b + 1, odd)):
                 at = (a * depths + d) * BLK
+                value = 1.5 * own[:, at : at + LANES].astype(F32) - 0.5 * cube
                 out[:, at : at + LANES] = value.astype(BF16)
 
 
-def join(got):
-    depths, width, lanes = got.shape
-    return call(join_kernel, out_shape=jax.ShapeDtypeStruct((width, depths * lanes), BF16))(got)
+def update(own, got):
+    return call(update_kernel, out_shape=jax.ShapeDtypeStruct(own.shape, BF16))(own, got)
 
 
 def shards(matrix, occupancy, filtering):
@@ -199,7 +244,13 @@
         ]
         return lax.ppermute(value, ("row", "col"), route)
 
-    def sum_over_row(right):
+    def parts_of(right):
+        [away] = terms_of(right, left, where, scale, own_rows, (1, 3), together=True)
+        near, both = swap_row(away, 1)
+        across, here = terms_of(right, left, where, scale, own_rows, (2, 0))
+        return here, near, across, both
+
+    def parts_added(right):
         [both] = terms_of(right, left, where, scale, own_rows, (3,))
         both = swap_row(both, 1)
         [across] = terms_of(right, left, where, scale, own_rows, (2,))
@@ -210,20 +261,29 @@
         across, here = lax.optimization_barrier((across, here))
         return here, across, swap_row(near, 1)
 
-    own = left_part(matrix, occupancy, depth.astype(jnp.int32)[None], depths)
-    moved = trade_x_and_row(own.astype(F16))
+    def trade_over_chip_and_depth(value):
+        groups = [
+            [r * depths + d for r in (core, core + 2) for d in range(depths)] for core in range(2)
+        ]
+        return lax.all_to_all(
+            value, ("row", "depth"), 0, 0, tiled=True, axis_index_groups=groups
+        )
+
+    piece = left_part(matrix, occupancy, depth.astype(jnp.int32)[None], depths)
+    moved = trade_x_and_row(piece.astype(F16))
     right = right_part(matrix, occupancy)
     mask = filter_mask(filtering, where, depths, local_rows // BLK, local_cols // BLK)
-    right, mask, moved = lax.optimization_barrier((right, mask, moved))
+    own = own_columns(matrix, occupancy, where)
+    right, mask, own, moved = lax.optimization_barrier((right, mask, own, moved))
     left = gather_col(gather_col(moved, ALONG_Z), ALONG_X).astype(BF16)
 
-    here, across, near = sum_over_row(right)
+    here, across, near = parts_added(right)
     square = sum(part.astype(F32) for part in (here, across, near)) * mask.astype(F32)
     square = square.astype(BF16).astype(F16)
     squares = lax.all_gather(square, "depth", axis=0).astype(BF16)
 
-    new = update(own, sum_over_row(squares)).reshape(depths, BLK, own_rows)
-    return join(lax.all_to_all(new, "depth", 0, 0, tiled=True)).T
+    parts = pack(parts_of(squares), where).reshape(2 * depths, BLK, own_rows)
+    return update(own, trade_over_chip_and_depth(parts)).T
 
 
 def solution(mesh):

time: 160 us -> 158 us (0.988)
  blocking collectives: 111 us -> 118 us
  waiting for transfers between devices: 14.8 us -> 7.98 us
  starting transfers between devices: 15.9 us -> 11.6 us
    ppermute x6 -> x4, waiting for transfers between devices: 9.45 us -> 4.81 us  [swap_row(): return lax.ppermute(value, 'row', [(r, r ^ bit) for r in range(rows)])]
    all_to_all x1, blocking collectives: 16.6 us -> 21.2 us  [trade_over_chip_and_depth(): lax.all_to_all(value, ('row', 'depth'), 0, 0, tiled=True, axis_index_grou...]
    ppermute x6 -> x4, starting transfers between devices: 12.1 us -> 7.93 us  [swap_row(): return lax.ppermute(value, 'row', [(r, r ^ bit) for r in range(rows)])]
    all_gather x2, blocking collectives: 63.4 us -> 65.6 us  [gather_col(): lax.all_gather(value, 'col', axis=0, tiled=True, axis_index_groups=groups)]
    ppermute x1, waiting for transfers between devices: 5.4 us -> 3.17 us  [trade_x_and_row(): return lax.ppermute(value, ('row', 'col'), route)]
    pallas_call x6 -> x5, Pallas kernels: 8.54 us -> 7.84 us  [terms_of(): call(functools.partial(terms_kernel, held, scale), flops=2 * rows * len(h...]
  transfers between devices with their start and end apart: 7 -> 5, of which waited for: 5 -> 4; matrix products, arithmetic and copies ran while one was open for 0% -> 0% of each run, Pallas kernels for 5% -> 4%
where the time goes in v2:
time: 158 us; the launch traced here: 157 us
  blocking collectives  118 us (75%)
  Pallas kernels  13.6 us (9%)
  starting transfers between devices  11.6 us (7%)
  waiting for transfers between devices  7.98 us (5%)
  local copies, waits for them, and re-layouts  3.22 us (2%)
  other arithmetic  2.53 us (2%)
    all_gather x2, blocking collectives, gather_col(): lax.all_gather(value, 'col', axis=0, tiled=True, axis_index_groups=groups)  65.6 us
    all_gather x1, blocking collectives, shards(): squares = lax.all_gather(square, 'depth', axis=0).astype(BF16)  31.2 us
    all_to_all x1, blocking collectives, trade_over_chip_and_depth(): lax.all_to_all(value, ('row', 'depth'), 0, 0, tiled=True, axis_index_grou...  21.2 us
    ppermute x4, starting transfers between devices, swap_row(): return lax.ppermute(value, 'row', [(r, r ^ bit) for r in range(rows)])  7.93 us
    pallas_call x5, Pallas kernels, terms_of(): call(functools.partial(terms_kernel, held, scale), flops=2 * rows * len(h...  7.84 us
    ppermute x4, waiting for transfers between devices, swap_row(): return lax.ppermute(value, 'row', [(r, r ^ bit) for r in range(rows)])  4.81 us
    ppermute x1, starting transfers between devices, trade_x_and_row(): return lax.ppermute(value, ('row', 'col'), route)  3.72 us
    unnamed x8, local copies, waits for them, and re-layouts  3.19 us
  transfers between devices with their start and end apart: 5, of which 4 were waited for; matrix products, arithmetic and copies ran while one was open for 0% of the time, Pallas kernels for 4%

profile of v2, /device:TPU:6, one launch (start us, length us, event | category | flops | bytes accessed | tf_op | source)
XLA Modules:
  0.0 157.2 jit_solution(9993479161485149223)
XLA Ops:
  0.0 1.9 %shard_map.40 = bf16[256,512]{1,0:T(8,128)(2,1)} custom-call(s32[1]{0:T(128)} %bitcast.1.where, s32[8,32]{1,0:T(8,128)} %bitcast.18, bf16[4,8,64,512]{3,2,1,0:T(8,128)(2,1)} %bitcast.13), custom_call_target="tpu_custom_call" | custom-call | bytes 1048576 | tf_op jit(solution)/shard_map/pallas_call | solution.py:51
  1.9 1.0 convert_element_type.36
  2.9 3.7 %collective-permute-start = (f16[256,512]{1,0:T(8,128)(2,1)S(1)}, f16[256,512]{1,0:T(8,128)(2,1)S(1)}, u32[]{:S(2)}, u32[]{:S(2)}) collective-permute-start(f16[256,512]{1,0:T(8,128)(2,1)S(1)} %convert_element_type.36), channel_id=1, source_target_pairs={{0,0},{8,8},{16,16},{24,24},{32,160},{40,168},{48,176},{56,184},{6... | collective-permute-start | bytes 786440 | tf_op jit(solution)/shard_map/ppermute | solution.py:245
  6.7 1.6 %copy-done = bf16[2048,512]{1,0:T(8,128)(2,1)S(1)} copy-done((bf16[2048,512]{1,0:T(8,128)(2,1)S(1)}, bf16[2048,512]{1,0:T(8,128)(2,1)}, u32[]{:S(2)}) %copy-start) | copy-done | bytes 2097176
  8.9 1.6 %copy-done.1 = bf16[2048,512]{1,0:T(8,128)(2,1)S(1)} copy-done((bf16[2048,512]{1,0:T(8,128)(2,1)S(1)}, bf16[2048,512]{1,0:T(8,128)(2,1)}, u32[]{:S(2)}) %copy-start.1) | copy-done | bytes 2097176
  10.5 0.8 shard_map.39.own
  11.3 0.9 shard_map.38
  12.2 3.2 %collective-permute-done = f16[256,512]{1,0:T(8,128)(2,1)S(1)} collective-permute-done((f16[256,512]{1,0:T(8,128)(2,1)S(1)}, f16[256,512]{1,0:T(8,128)(2,1)S(1)}, u32[]{:S(2)}, u32[]{:S(2)}) %collective-permute-start) | collective-permute-done | bytes 262176 | tf_op jit(solution)/shard_map/ppermute | solution.py:245
  15.4 28.2 %all-gather.4 = f16[1024,512]{1,0:T(8,128)(2,1)S(1)} all-gather(f16[256,512]{1,0:T(8,128)(2,1)S(1)} %collective-permute-done), channel_id=1, replica_groups={{0,8,16,24},{32,40,48,56},{64,72,80,88},{96,104,112,120},{1,9,17,25},{3..., dimensions={0}, use_global_device_ids=true | all-gather | bytes 1310720 | tf_op jit(solution)/shard_map/all_gather | solution.py:234
  43.6 37.4 %all-gather.5 = f16[4096,512]{1,0:T(8,128)(2,1)S(1)} all-gather(f16[1024,512]{1,0:T(8,128)(2,1)S(1)} %all-gather.4), channel_id=1, replica_groups={{0,32,64,96},{8,40,72,104},{16,48,80,112},{24,56,88,120},{1,33,65,97},{..., dimensions={0}, use_global_device_ids=true | all-gather | bytes 5242880 | tf_op jit(solution)/shard_map/all_gather | solution.py:234
  81.0 0.8 convert_element_type.37.left
  81.8 1.2 shard_map.42
  83.0 1.9 %collective-permute-start.1 = (bf16[256,512]{1,0:T(8,128)(2,1)S(1)}, bf16[256,512]{1,0:T(8,128)(2,1)S(1)}, u32[]{:S(2)}, u32[]{:S(2)}) collective-permute-start(bf16[256,512]{1,0:T(8,128)(2,1)S(1)} %shard_map.42), channel_id=1, source_target_pairs={{0,128},{128,0},{256,384},{384,256},{1,129},{129,1},{257,385},{385... | collective-permute-start | bytes 786440 | tf_op jit(solution)/shard_map/ppermute | solution.py:237
  85.0 1.2 shard_map.41
  86.5 1.9 %collective-permute-start.2 = (bf16[256,512]{1,0:T(8,128)(2,1)S(1)}, bf16[256,512]{1,0:T(8,128)(2,1)S(1)}, u32[]{:S(2)}, u32[]{:S(2)}) collective-permute-start(bf16[256,512]{1,0:T(8,128)(2,1)S(1)} %add_convert_fusion), channel_id=1, source_target_pairs={{0,256},{128,384},{256,0},{384,128},{1,257},{129,385},{257,1},{385... | collective-permute-start | bytes 786440 | tf_op jit(solution)/shard_map/ppermute | solution.py:237
  88.5 1.8 %shard_map.43 = (bf16[256,512]{1,0:T(8,128)(2,1)S(1)}, bf16[256,512]{1,0:T(8,128)(2,1)S(1)}) custom-call(s32[3]{0:T(128)S(1)} %pad_add_fusion.where, bf16[2048,512]{1,0:T(8,128)(2,1)S(1)} %shard_map.37.right, bf16[4096,512]{1,0:T(8,128)(2,1)S(1)} %convert_element_type.37.left), custom_call_target="tpu_custom_call" | custom-call | flops 1073741824 | bytes 4718592 | tf_op jit(solution)/shard_map/pallas_call | solution.py:144
  90.3 2.2 %collective-permute-start.3 = (bf16[256,512]{1,0:T(8,128)(2,1)S(1)}, bf16[256,512]{1,0:T(8,128)(2,1)S(1)}, u32[]{:S(2)}, u32[]{:S(2)}) collective-permute-start(bf16[256,512]{1,0:T(8,128)(2,1)S(1)} %get-tuple-element.25), channel_id=1, source_target_pairs={{0,128},{128,0},{256,384},{384,256},{1,129},{129,1},{257,385},{385... | collective-permute-start | bytes 786440 | tf_op jit(solution)/shard_map/ppermute | solution.py:237
  92.4 4.5 %collective-permute-done.2 = bf16[256,512]{1,0:T(8,128)(2,1)S(1)} collective-permute-done((bf16[256,512]{1,0:T(8,128)(2,1)S(1)}, bf16[256,512]{1,0:T(8,128)(2,1)S(1)}, u32[]{:S(2)}, u32[]{:S(2)}) %collective-permute-start.2) | collective-permute-done | bytes 262176 | tf_op jit(solution)/shard_map/ppermute | solution.py:237
  97.1 31.2 %all-gather.6 = f16[2048,512]{1,0:T(8,128)(2,1)S(1)} all-gather(f16[256,512]{1,0:T(8,128)(2,1)S(1)} %fusion), channel_id=2, replica_groups=mesh['row'=4,'col'=16,'depth'=8] {'depth'}, dimensions={0}, use_global_device_ids=true | all-gather | bytes 2359296 | tf_op jit(solution)/shard_map/all_gather | solution.py:283
  128.7 1.8 %shard_map.45 = bf16[2,256,512]{2,1,0:T(8,128)(2,1)S(1)} custom-call(s32[3]{0:T(128)S(1)} %pad_add_fusion.where, bf16[8,256,512]{2,1,0:T(8,128)(2,1)S(1)} %bitcast.15, bf16[4096,512]{1,0:T(8,128)(2,1)S(1)} %convert_element_type.37.left), custom_call_target="tpu_custom_call" | custom-call | flops 1073741824 | bytes 4718592 | tf_op jit(solution)/shard_map/pallas_call | solution.py:144
  130.5 1.9 %collective-permute-start.4 = (bf16[2,256,512]{2,1,0:T(8,128)(2,1)S(1)}, bf16[2,256,512]{2,1,0:T(8,128)(2,1)S(1)}, u32[]{:S(2)}, u32[]{:S(2)}) collective-permute-start(bf16[2,256,512]{2,1,0:T(8,128)(2,1)S(1)} %shard_map.45), channel_id=1, source_target_pairs={{0,128},{128,0},{256,384},{384,256},{1,129},{129,1},{257,385},{385... | collective-permute-start | bytes 1572872 | tf_op jit(solution)/shard_map/ppermute | solution.py:237
  132.4 1.8 %shard_map.44 = (bf16[256,512]{1,0:T(8,128)(2,1)S(1)}, bf16[256,512]{1,0:T(8,128)(2,1)S(1)}) custom-call(s32[3]{0:T(128)S(1)} %pad_add_fusion.where, bf16[8,256,512]{2,1,0:T(8,128)(2,1)S(1)} %bitcast.16, bf16[4096,512]{1,0:T(8,128)(2,1)S(1)} %convert_element_type.37.left), custom_call_target="tpu_custom_call" | custom-call | flops 1073741824 | bytes 4718592 | tf_op jit(solution)/shard_map/pallas_call | solution.py:144
  135.1 21.2 %all_to_all.5.got = bf16[16,64,256]{2,1,0:T(8,128)(2,1)S(1)} all-to-all(bf16[16,64,256]{2,1,0:T(8,128)(2,1)S(1)} %bitcast.17), channel_id=1, replica_groups={{0,1,2,3,4,5,6,7,256,257,258,259,260,261,262,263},{128,129,130,131,132,..., dimensions={0} | all-to-all | bytes 1048576 | tf_op jit(solution)/shard_map/all_to_all | solution.py:268
  156.3 0.9 shard_map.47
  (16 shorter events, 2.4 us)
Async XLA Ops:
  0.0 6.6 %copy-start.3 = (s32[32,8]{0,1:T(8,128)S(1)}, s32[32,8]{0,1:T(8,128)}, u32[]{:S(2)}) copy-start(s32[32,8]{0,1:T(8,128)} %param.4) | copy-start | bytes 3076
  2.9 12.4 %collective-permute-start = (f16[256,512]{1,0:T(8,128)(2,1)S(1)}, f16[256,512]{1,0:T(8,128)(2,1)S(1)}, u32[]{:S(2)}, u32[]{:S(2)}) collective-permute-start(f16[256,512]{1,0:T(8,128)(2,1)S(1)} %convert_element_type.36), channel_id=1, source_target_pairs={{0,0},{8,8},{16,16},{24,24},{32,160},{40,168},{48,176},{56,184},{6... | collective-permute-start | bytes 786440 | tf_op jit(solution)/shard_map/ppermute | solution.py:245
  6.7 1.6 %copy-start = (bf16[2048,512]{1,0:T(8,128)(2,1)S(1)}, bf16[2048,512]{1,0:T(8,128)(2,1)}, u32[]{:S(2)}) copy-start(bf16[2048,512]{1,0:T(8,128)(2,1)} %rows.1) | copy-start | bytes 6291460
  8.2 3.1 %copy-start.2 = (s32[128,128]{1,0:T(8,128)S(1)}, s32[128,128]{1,0:T(8,128)}, u32[]{:S(2)}) copy-start(s32[128,128]{1,0:T(8,128)} %filtering.1) | copy-start | bytes 196612
  8.9 1.6 %copy-start.1 = (bf16[2048,512]{1,0:T(8,128)(2,1)S(1)}, bf16[2048,512]{1,0:T(8,128)(2,1)}, u32[]{:S(2)}) copy-start(bf16[2048,512]{1,0:T(8,128)(2,1)} %rows.1) | copy-start | bytes 6291460
  83.0 3.4 %collective-permute-start.1 = (bf16[256,512]{1,0:T(8,128)(2,1)S(1)}, bf16[256,512]{1,0:T(8,128)(2,1)S(1)}, u32[]{:S(2)}, u32[]{:S(2)}) collective-permute-start(bf16[256,512]{1,0:T(8,128)(2,1)S(1)} %shard_map.42), channel_id=1, source_target_pairs={{0,128},{128,0},{256,384},{384,256},{1,129},{129,1},{257,385},{385... | collective-permute-start | bytes 786440 | tf_op jit(solution)/shard_map/ppermute | solution.py:237
  86.5 10.4 %collective-permute-start.2 = (bf16[256,512]{1,0:T(8,128)(2,1)S(1)}, bf16[256,512]{1,0:T(8,128)(2,1)S(1)}, u32[]{:S(2)}, u32[]{:S(2)}) collective-permute-start(bf16[256,512]{1,0:T(8,128)(2,1)S(1)} %add_convert_fusion), channel_id=1, source_target_pairs={{0,256},{128,384},{256,0},{384,128},{1,257},{129,385},{257,1},{385... | collective-permute-start | bytes 786440 | tf_op jit(solution)/shard_map/ppermute | solution.py:237
  90.3 6.6 %collective-permute-start.3 = (bf16[256,512]{1,0:T(8,128)(2,1)S(1)}, bf16[256,512]{1,0:T(8,128)(2,1)S(1)}, u32[]{:S(2)}, u32[]{:S(2)}) collective-permute-start(bf16[256,512]{1,0:T(8,128)(2,1)S(1)} %get-tuple-element.25), channel_id=1, source_target_pairs={{0,128},{128,0},{256,384},{384,256},{1,129},{129,1},{257,385},{385... | collective-permute-start | bytes 786440 | tf_op jit(solution)/shard_map/ppermute | solution.py:237
  130.5 3.8 %collective-permute-start.4 = (bf16[2,256,512]{2,1,0:T(8,128)(2,1)S(1)}, bf16[2,256,512]{2,1,0:T(8,128)(2,1)S(1)}, u32[]{:S(2)}, u32[]{:S(2)}) collective-permute-start(bf16[2,256,512]{2,1,0:T(8,128)(2,1)S(1)} %shard_map.45), channel_id=1, source_target_pairs={{0,128},{128,0},{256,384},{384,256},{1,129},{129,1},{257,385},{385... | collective-permute-start | bytes 1572872 | tf_op jit(solution)/shard_map/ppermute | solution.py:237
